TPU v7x, 256 devices: a whole 4x4x8 slice. The times are simulated.
256 devices in a mesh: segment: 2 (over x_lo), frame: 8 (over z), row: 16 (over y, x_hi, core).
Axes of the slice: x: 4 (x_hi: 2, x_lo: 2; x = x_hi * 2 + x_lo), y: 4, z: 8, core: 2. Of those that a mesh axis runs over, the one named last changes fastest.
Arguments:
- stream: bfloat16 [2, 16, 32, 32, 2048], P('segment', 'frame', 'row'), may hold values from -45 to 45
- mixer_gain: float32 [2, 2048], P('segment'), may hold values from 0.1 to 1.9
- spectrum: bfloat16 [2, 2, 32, 32, 2048], P('segment', None, 'row'), may hold values from -6 to 6
- mlp_gain: float32 [2, 2048], P('segment'), may hold values from 0.1 to 1.9
- gate_weight: bfloat16 [2, 2048, 8192], P('segment', 'frame', 'row'), may hold values from -0.125 to 0.125
- up_weight: bfloat16 [2, 2048, 8192], P('segment', 'frame', 'row'), may hold values from -0.125 to 0.125
- down_weight: bfloat16 [2, 2048, 8192], P('segment', 'frame', 'row'), may hold values from -0.0625 to 0.0625
Outputs:
- result: bfloat16 [2, 16, 32, 32, 2048], P('segment', 'frame', 'row')
All inputs are finite; a program needn't handle non-finite values.
Results may differ from a plain program's by a relative error of at most 0.013.
Values may be sent and summed in bfloat16 or wider, within the bound.
A program may use at most 128 MiB of HBM per device.

v0:
```python
import math

import jax
import jax.numpy as jnp
from jax import lax
from jax.sharding import PartitionSpec as P


def from_behind(value, axis, by):
    devices = lax.axis_size(axis)
    return lax.ppermute(value, axis, [(i, (i + by) % devices) for i in range(devices)])


def rms_scale(values, norm_gain):
    widened = values.astype(jnp.float32)
    mean_square = jnp.mean(widened * widened, axis=-1, keepdims=True)
    return widened * lax.rsqrt(mean_square + 1e-05) * norm_gain


def cosine_sine(length):
    indices = jnp.arange(length, dtype=jnp.int32)
    products = indices[:, None] * indices[None, :] % length
    angles = products.astype(jnp.float32) * (2.0 * math.pi / length)
    return (jnp.cos(angles).astype(jnp.bfloat16), jnp.sin(angles).astype(jnp.bfloat16))


def dft_tables(height, width):
    cosine_cols, sine_cols = cosine_sine(width)
    cosine_rows, sine_rows = cosine_sine(height)
    forward_cols = jnp.stack((cosine_cols, -sine_cols), axis=1)
    forward_rows = jnp.stack(
        (jnp.stack((cosine_rows, -sine_rows), axis=1), jnp.stack((sine_rows, cosine_rows), axis=1)),
        axis=1,
    )
    inverse_rows = jnp.stack(
        (jnp.stack((cosine_rows, sine_rows), axis=1), jnp.stack((-sine_rows, cosine_rows), axis=1)),
        axis=1,
    ).astype(jnp.float32)
    inverse_cols = jnp.stack((cosine_cols, -sine_cols), axis=0)
    return (forward_cols, forward_rows, inverse_rows, inverse_cols)


def column_transform(normed, forward_cols):
    return jnp.einsum(
        "fhwd,wck->fhckd", normed, forward_cols, preferred_element_type=jnp.float32
    ).astype(jnp.bfloat16)


def row_filter(col_pencils, filt, forward_rows, inverse_rows):
    full_spec = jnp.einsum(
        "fhckd,hcem->fekmd", col_pencils, forward_rows, preferred_element_type=jnp.float32
    )
    filt_wide = filt.astype(jnp.float32)
    real_part = full_spec[:, 0] * filt_wide[0] - full_spec[:, 1] * filt_wide[1]
    imag_part = full_spec[:, 0] * filt_wide[1] + full_spec[:, 1] * filt_wide[0]
    filtered = jnp.stack((real_part, imag_part), axis=1)
    back = jnp.einsum(
        "fckmd,mceh->fehkd",
        filtered,
        inverse_rows,
        precision=lax.Precision.HIGHEST,
        preferred_element_type=jnp.float32,
    )
    return back.astype(jnp.bfloat16)


def inverse_transform(back_rows, inverse_cols):
    return jnp.einsum(
        "fehkd,ekw->fhwd", back_rows, inverse_cols, preferred_element_type=jnp.float32
    )


def body(stream, mixer_gain, spectrum, mlp_gain, gate_weight, up_weight, down_weight):
    local = stream[0]
    frames, rows_here, width, depth = local.shape
    height = rows_here * lax.axis_size("row")
    forward_cols, forward_rows, inverse_rows, inverse_cols = dft_tables(height, width)
    normed = rms_scale(local, mixer_gain[0]).astype(jnp.bfloat16)
    scale_back = 1.0 / (height * width)
    col_spec = column_transform(normed, forward_cols)
    col_pencils = lax.all_to_all(col_spec, "row", split_axis=3, concat_axis=1, tiled=True)
    back = row_filter(col_pencils, spectrum[0], forward_rows, inverse_rows)
    back_rows = lax.all_to_all(back, "row", split_axis=2, concat_axis=3, tiled=True)
    conv = inverse_transform(back_rows, inverse_cols) * scale_back
    mixed = (local.astype(jnp.float32) + normed.astype(jnp.float32) * conv).astype(jnp.bfloat16)
    received = from_behind(mixed, "segment", 1)
    normed_next = rms_scale(received, mlp_gain[0]).astype(jnp.bfloat16)
    tokens_all = lax.all_gather(jnp.swapaxes(normed_next, 0, 1), "row", axis=0, tiled=True)
    gate_full, up_full, down_full = (
        lax.all_gather(gate_weight[0], "frame", axis=0, tiled=True),
        lax.all_gather(up_weight[0], "frame", axis=0, tiled=True),
        lax.all_gather(down_weight[0], "frame", axis=0, tiled=True),
    )
    flat_tokens = tokens_all.reshape(-1, depth)
    gate = jnp.dot(flat_tokens, gate_full, preferred_element_type=jnp.float32)
    upward = jnp.dot(flat_tokens, up_full, preferred_element_type=jnp.float32)
    hidden = (jax.nn.silu(gate) * upward).astype(jnp.bfloat16)
    summed = lax.psum_scatter(
        lax.dot_general(
            hidden, down_full, (((1,), (1,)), ((), ())), preferred_element_type=jnp.float32
        ).astype(jnp.bfloat16),
        "row",
        scatter_dimension=0,
        tiled=True,
    ).astype(jnp.float32)
    summed = jnp.swapaxes(summed.reshape(rows_here, frames, width, depth), 0, 1)
    output_block = (received.astype(jnp.float32) + summed).astype(jnp.bfloat16)
    return output_block[None]


def solution(mesh):
    return jax.shard_map(
        body,
        mesh=mesh,
        in_specs=(
            P("segment", "frame", "row", None, None),
            P("segment", None),
            P("segment", None, "row", None, None),
            P("segment", None),
            P("segment", "frame", "row"),
            P("segment", "frame", "row"),
            P("segment", "frame", "row"),
        ),
        out_specs=P("segment", "frame", "row", None, None),
        check_vma=False,
    )
```

profile of v0, /device:TPU:1, one launch (start us, length us, event | category | flops | bytes accessed | tf_op | source)
XLA Modules:
  0.0 406.5 jit_solution(13668435384855902816)
XLA Ops:
  6.5 0.1 cosine_convert_fusion
  6.6 0.1 fusion.49
  6.7 1.2 fusion.18
  7.9 1.5 fusion.1
  9.5 0.0 copy-start.1
  9.5 2.1 copy.20
  11.6 8.4 %all-to-all-start = ((bf16[2,2,2,32,2048]{4,1,0,2,3:T(2,128)(2,1)}), bf16[2,2,2,32,2048]{4,1,0,2,3:T(2,128)(2,1)S(1)}, u32[]{:S(2)}, u32[]{:S(2)}) async-start(bf16[2,2,2,32,2048]{4,1,0,2,3:T(2,128)(2,1)} %copy.20), calls=%async_computation | async-start | bytes 2097152 | tf_op jit(solution)/shard_map/all_to_all | solution.py:81
  20.0 0.0 copy-done.1
  20.0 0.1 convert_element_type.166
  20.1 0.1 sine_convert_fusion
  20.3 0.1 slice_bitcast_fusion.1
  20.3 16.9 %all-to-all-done = bf16[2,2,2,32,2048]{4,1,0,2,3:T(2,128)(2,1)S(1)} async-done(((bf16[2,2,2,32,2048]{4,1,0,2,3:T(2,128)(2,1)}), bf16[2,2,2,32,2048]{4,1,0,2,3:T(2,128)(2,1)S(1)}, u32[]{:S(2)}, u32[]{:S(2)}) %all-to-all-start) | async-done | bytes 1048608 | tf_op jit(solution)/shard_map/all_to_all | solution.py:81
  37.2 0.8 copy.54
  38.1 0.4 reshape.200
  38.5 0.5 convolution_bitcast_fusion
  39.0 0.3 multiply_subtract_fusion
  39.3 1.2 fusion.6
  40.5 2.1 copy.25
  42.6 4.3 %all-to-all-start.1 = ((bf16[2,2,32,2,2048]{4,3,0,1,2:T(2,128)(2,1)}), bf16[2,2,32,2,2048]{4,3,0,1,2:T(2,128)(2,1)S(1)}, u32[]{:S(2)}, u32[]{:S(2)}) async-start(bf16[2,2,32,2,2048]{4,3,0,1,2:T(2,128)(2,1)} %copy.25), calls=%async_computation.1 | async-start | bytes 2097152 | tf_op jit(solution)/shard_map/all_to_all | solution.py:83
  47.0 0.0 all-gather.8.cloned.1.call-start
  47.0 0.1 cosine_convert_fusion.1
  47.1 0.1 fusion.48
  47.2 17.1 %all-to-all-done.1 = bf16[2,2,32,2,2048]{4,3,0,1,2:T(2,128)(2,1)S(1)} async-done(((bf16[2,2,32,2,2048]{4,3,0,1,2:T(2,128)(2,1)}), bf16[2,2,32,2,2048]{4,3,0,1,2:T(2,128)(2,1)S(1)}, u32[]{:S(2)}, u32[]{:S(2)}) %all-to-all-start.1) | async-done | bytes 1048608 | tf_op jit(solution)/shard_map/all_to_all | solution.py:83
  64.2 0.0 copy-start
  64.2 0.0 copy-start.2
  64.2 0.8 copy.53
  65.1 0.0 copy-start.3
  65.1 0.4 all_to_all.33
  65.6 0.0 copy-done
  65.6 0.0 copy-done.2
  65.6 0.5 fusion.7
  66.1 0.5 collective-permute-start
  66.5 12.1 %collective-permute-done = bf16[2,2,32,2048]{3,2,1,0:T(8,128)(2,1)S(1)} collective-permute-done((bf16[2,2,32,2048]{3,2,1,0:T(8,128)(2,1)S(1)}, bf16[2,2,32,2048]{3,2,1,0:T(8,128)(2,1)S(1)}, u32[]{:S(2)}, u32[]{:S(2)}) %collective-permute-start) | collective-permute-done | bytes 524320 | tf_op jit(solution)/shard_map/ppermute | solution.py:11
  78.7 0.2 fusion.14
  78.9 0.0 copy-done.3
  78.9 1.0 fusion.22
  79.9 0.0 all-gather.8.cloned.1.call-update
  79.9 0.0 all-gather.10.cloned.1.call-start
  79.9 0.7 all-gather.10.cloned.1.call-update
  80.7 0.0 all-gather.12.cloned.1.call-start
  80.7 0.7 all-gather.12.cloned.1.call-update
  81.4 0.0 all-gather.14.cloned.1.call-start
  81.4 0.5 all-gather.14.cloned.1.call-update
  82.0 0.2 reduce-scatter.2.cloned.1.call-start
  82.2 76.5 %all-gather.8.cloned.1.call-done = bf16[32,2,32,2048]{3,2,0,1:T(8,128)(2,1)} async-done(((bf16[2,2,32,2048]{3,2,0,1:T(8,128)(2,1)}), bf16[32,2,32,2048]{3,2,0,1:T(8,128)(2,1)}) %all-gather.8.cloned.1.call-update) | async-done | bytes 8388624 | tf_op jit(solution)/shard_map/all_gather | solution.py:88
  158.6 8.3 %copy.27 = bf16[32,2,32,2048]{3,2,1,0:T(8,128)(2,1)} copy(bf16[32,2,32,2048]{3,2,0,1:T(8,128)(2,1)} %all-gather.8.cloned.1.call-done) | data formatting | bytes 16777216 | tf_op jit(solution)/shard_map/all_gather | solution.py:88
  166.9 28.4 %all-gather.10.cloned.1.call-done = bf16[1,2048,512]{2,1,0:T(8,128)(2,1)} async-done(((bf16[1,256,512]{2,1,0:T(8,128)(2,1)}), bf16[1,2048,512]{2,1,0:T(8,128)(2,1)}) %all-gather.10.cloned.1.call-update) | async-done | bytes 2097168 | tf_op jit(solution)/shard_map/all_gather | solution.py:90
  195.3 10.5 %fusion.10 = f32[2048,512]{1,0:T(8,128)} fusion(bf16[2048,2048]{1,0:T(8,128)(2,1)} %bitcast.118, bf16[1,2048,512]{2,1,0:T(8,128)(2,1)} %all-gather.10.cloned.1.call-done), kind=kOutput, calls=%fused_computation.17 | convolution fusion | flops 4294967296 | bytes 14680064 | tf_op jit(solution)/shard_map/dot_general | solution.py:95
  205.8 31.0 %all-gather.12.cloned.1.call-done = bf16[1,2048,512]{2,1,0:T(8,128)(2,1)} async-done(((bf16[1,256,512]{2,1,0:T(8,128)(2,1)}), bf16[1,2048,512]{2,1,0:T(8,128)(2,1)}) %all-gather.12.cloned.1.call-update) | async-done | bytes 2097168 | tf_op jit(solution)/shard_map/all_gather | solution.py:91
  236.8 10.4 %multiply_convert_fusion = bf16[2048,512]{1,0:T(8,128)(2,1)S(1)} fusion(f32[2048,512]{1,0:T(8,128)} %fusion.10, bf16[2048,2048]{1,0:T(8,128)(2,1)} %bitcast.119, bf16[1,2048,512]{2,1,0:T(8,128)(2,1)} %all-gather.12.cloned.1.call-done), kind=kOutput, calls=%fused_computation.1 | convolution fusion | flops 4301258752 | bytes 16777216 | tf_op jit(solution)/shard_map/dot_general | solution.py:96
  247.2 30.9 %all-gather.14.cloned.1.call-done = bf16[1,2048,512]{2,1,0:T(8,128)(2,1)} async-done(((bf16[1,256,512]{2,1,0:T(8,128)(2,1)}), bf16[1,2048,512]{2,1,0:T(8,128)(2,1)}) %all-gather.14.cloned.1.call-update) | async-done | bytes 2097168 | tf_op jit(solution)/shard_map/all_gather | solution.py:92
  278.1 8.3 %convolution_convert_fusion = bf16[2048,2048]{1,0:T(8,128)(2,1)} fusion(bf16[2048,512]{1,0:T(8,128)(2,1)S(1)} %multiply_convert_fusion, bf16[1,2048,512]{2,1,0:T(8,128)(2,1)} %all-gather.14.cloned.1.call-done), kind=kOutput, calls=%fused_computation | convolution fusion | flops 4299161600 | bytes 12582912 | tf_op jit(solution)/shard_map/dot_general | solution.py:99
  286.4 0.0 reduce-scatter.2.cloned.1.call-update
  286.5 111.5 %reduce-scatter.2.cloned.1.call-done = bf16[128,2048]{1,0:T(8,128)(2,1)} async-done(((bf16[2048,2048]{1,0:T(8,128)(2,1)}), bf16[128,2048]{1,0:T(8,128)(2,1)}) %reduce-scatter.2.cloned.1.call-update) | async-done | bytes 524304 | tf_op jit(solution)/shard_map/reduce_scatter | solution.py:98
  398.0 2.0 fusion.21
  (4 shorter events, 0.0 us)
Async XLA Ops:
  9.5 10.5 %copy-start.1 = (bf16[1,2,2,32,2048]{4,3,2,1,0:T(8,128)(2,1)S(1)}, bf16[1,2,2,32,2048]{4,3,2,1,0:T(8,128)(2,1)}, u32[]{:S(2)}) copy-start(bf16[1,2,2,32,2048]{4,3,2,1,0:T(8,128)(2,1)} %param.9) | copy-start | bytes 1572868
  11.6 25.7 %all-to-all-start = ((bf16[2,2,2,32,2048]{4,1,0,2,3:T(2,128)(2,1)}), bf16[2,2,2,32,2048]{4,1,0,2,3:T(2,128)(2,1)S(1)}, u32[]{:S(2)}, u32[]{:S(2)}) async-start(bf16[2,2,2,32,2048]{4,1,0,2,3:T(2,128)(2,1)} %copy.20), calls=%async_computation | async-start | bytes 2097152 | tf_op jit(solution)/shard_map/all_to_all | solution.py:81
  42.6 21.6 %all-to-all-start.1 = ((bf16[2,2,32,2,2048]{4,3,0,1,2:T(2,128)(2,1)}), bf16[2,2,32,2,2048]{4,3,0,1,2:T(2,128)(2,1)S(1)}, u32[]{:S(2)}, u32[]{:S(2)}) async-start(bf16[2,2,32,2,2048]{4,3,0,1,2:T(2,128)(2,1)} %copy.25), calls=%async_computation.1 | async-start | bytes 2097152 | tf_op jit(solution)/shard_map/all_to_all | solution.py:83
  47.0 111.7 %all-gather.8.cloned.1.call-start = ((), (), s32[]{:S(2)}) async-start(), calls=%async_computation.3 | async-start | bytes 8912896 | tf_op jit(solution)/shard_map/all_gather | solution.py:88
  64.2 1.3 copy-start
  64.2 1.3 copy-start.2
  65.1 13.8 %copy-start.3 = (f32[1,2048]{1,0:T(1,128)S(1)}, f32[1,2048]{1,0:T(1,128)}, u32[]{:S(2)}) copy-start(f32[1,2048]{1,0:T(1,128)} %param.10) | copy-start | bytes 24580
  66.1 12.6 %collective-permute-start = (bf16[2,2,32,2048]{3,2,1,0:T(8,128)(2,1)S(1)}, bf16[2,2,32,2048]{3,2,1,0:T(8,128)(2,1)S(1)}, u32[]{:S(2)}, u32[]{:S(2)}) collective-permute-start(bf16[2,2,32,2048]{3,2,1,0:T(8,128)(2,1)S(1)} %fusion.7), channel_id=1, source_target_pairs={{0,128},{128,0},{1,129},{129,1},{2,130},{130,2},{3,131},{131,3},{4... | collective-permute-start | bytes 1572872 | tf_op jit(solution)/shard_map/ppermute | solution.py:11
  79.9 115.4 %all-gather.10.cloned.1.call-start = ((), (), s32[]{:S(2)}) async-start(), calls=%async_computation.5 | async-start | bytes 2359296 | tf_op jit(solution)/shard_map/all_gather | solution.py:90
  80.7 156.1 %all-gather.12.cloned.1.call-start = ((), (), s32[]{:S(2)}) async-start(), calls=%async_computation.6 | async-start | bytes 2359296 | tf_op jit(solution)/shard_map/all_gather | solution.py:91
  81.4 196.7 %all-gather.14.cloned.1.call-start = ((), (), s32[]{:S(2)}) async-start(), calls=%async_computation.7 | async-start | bytes 2359296 | tf_op jit(solution)/shard_map/all_gather | solution.py:92
  82.0 316.0 %reduce-scatter.2.cloned.1.call-start = ((), (), s32[]{:S(2)}) async-start(), calls=%async_computation.4 | async-start | bytes 8912896 | tf_op jit(solution)/shard_map/reduce_scatter | solution.py:98
Sparse Core Ops, SparseCore 0:
  80.0 78.5 all-gather.7
  160.4 34.8 all-gather.9
  197.1 39.6 all-gather.11
  238.4 39.6 all-gather.13
  286.6 111.3 reduce-scatter.1
where the time goes:
time: 407 us; the launch traced here: 406 us
  waiting for transfers between devices  326 us (80%)
  matrix products  32.9 us (8%)
  local copies, waits for them, and re-layouts  15.1 us (4%)
  starting transfers between devices  13.6 us (3%)
  between operations  13.3 us (3%)
  other arithmetic  5.24 us (1%)
    reduce_scatter x1, waiting for transfers between devices, body(): lax.psum_scatter(lax.dot_general(hidden, down_full, (((1,), (1,)), ((), (...  112 us
    all_gather x1, waiting for transfers between devices, body(): lax.all_gather(jnp.swapaxes(normed_next, 0, 1), 'row', axis=0, tiled=True)  76.5 us
    all_gather x1, waiting for transfers between devices, body(): lax.all_gather(up_weight[0], 'frame', axis=0, tiled=True)  31 us
    all_gather x1, waiting for transfers between devices, body(): lax.all_gather(down_weight[0], 'frame', axis=0, tiled=True)  30.9 us
    all_gather x1, waiting for transfers between devices, body(): lax.all_gather(gate_weight[0], 'frame', axis=0, tiled=True)  28.4 us
    all_to_all x1, waiting for transfers between devices, body(): lax.all_to_all(back, 'row', split_axis=2, concat_axis=3, tiled=True)  17.1 us
    all_to_all x1, waiting for transfers between devices, body(): lax.all_to_all(col_spec, 'row', split_axis=3, concat_axis=1, tiled=True)  16.9 us
    ppermute x1, waiting for transfers between devices, from_behind(): lax.ppermute(value, axis, [(i, (i + by) % devices) for i in range(devices)])  12.1 us
  transfers between devices with their start and end apart: 8, of which 8 were waited for; matrix products, arithmetic and copies ran while one was open for 7% of the time, Pallas kernels for 0%

commit v1 on v0

v1 whole, which is shorter than its diff:
```python
import functools
import math

import jax
import jax.numpy as jnp
import numpy as np
from jax import lax
from jax.experimental import pallas as pl
from jax.experimental.pallas import tpu as pltpu
from jax.sharding import PartitionSpec as P

MESH = pl.DeviceIdType.MESH
BF16, F32 = jnp.bfloat16, jnp.float32

N_ROW, N_Y, N_Z = 16, 4, 8
FRAMES = 2
BLOCK = 64
TOKENS = N_ROW * BLOCK
LANES = 128
D, HID, WROWS = 2048, 512, 256
CHUNKS = 4
STEPS = FRAMES * CHUNKS
CCOLS = D // CHUNKS


def tables():
    n = 32
    index = np.arange(n)
    angle = (index[:, None] * index[None, :] % n) * (2.0 * math.pi / n)
    cos, sin = np.cos(angle), np.sin(angle)
    cos[np.abs(cos) < 1e-9] = 0.0
    sin[np.abs(sin) < 1e-9] = 0.0
    eye4, eye8 = np.eye(4), np.eye(8)
    fwd = np.stack((cos, -sin))
    col = np.einsum("cwk,hg->kchgw", fwd, eye8).reshape(512, 256)
    mix = np.empty((2, 2, n, n))
    mix[0, 0], mix[0, 1], mix[1, 0], mix[1, 1] = cos, -sin, sin, cos
    row = np.einsum("cejhm,kl->ekmjlch", mix.reshape(2, 2, 4, 8, n), eye4).reshape(256, 256)
    inv = np.empty((2, 2, n, n))
    inv[0, 0], inv[0, 1], inv[1, 0], inv[1, 1] = cos, sin, -sin, cos
    irow = np.einsum("cemah,kl->ahkeclm", inv.reshape(2, 2, n, 8, 4), eye4).reshape(256, 256)
    icol = np.einsum("eakw,hg->hwagke", fwd.reshape(2, 8, 4, n), eye4).reshape(128, 256)
    return tuple(jnp.asarray(t, BF16) for t in (col, row, irow, icol))


def kernel(
    stream, mixer_gain, spectrum, mlp_gain, gate_w, up_w, down_w,
    t_col, t_row, t_irow, t_icol,
    out,
    own_stream, rx_stream, rx_spec, aux_tx, aux_rx, rs_full, normed, col_buf, back_buf,
    full, wgu, wd, tok, hid,
    part, sib_tx, sib_rx,
    x1_tx, x1_rx, y2_tx, y2_rx, y3_tx, y3_rx, x4_tx, x4_rx, y5_tx, y5_rx,
    loc, a2a_s, a2a_r, zs, zr, ags, agr, rss, rsr,
):
    seg, z, me = lax.axis_index("segment"), lax.axis_index("frame"), lax.axis_index("row")
    core, xh, y = me % 2, (me // 2) % 2, me // 4
    row_of = lambda yy, xx, cc: (yy * 2 + xx) * 2 + cc
    ym, yp, y2 = (y + 3) % 4, (y + 1) % 4, (y + 2) % 4
    zm, zp = (z + 7) % 8, (z + 1) % 8
    to_yp, to_ym = (seg, z, row_of(yp, xh, core)), (seg, z, row_of(ym, xh, core))
    to_x, to_sib = (seg, z, row_of(y, 1 - xh, core)), (seg, z, row_of(y, xh, 1 - core))
    to_zp, to_zm = (seg, zp, me), (seg, zm, me)

    def remote(src, dst, ssem, rsem, to):
        return pltpu.make_async_remote_copy(
            src_ref=src, dst_ref=dst, send_sem=ssem, recv_sem=rsem, device_id=to, device_id_type=MESH
        )

    load_stream = pltpu.make_async_copy(stream, own_stream, loc.at[0])
    load_stream.start()
    my_rows = pl.ds(pl.multiple_of(z * WROWS, WROWS), WROWS)
    own_w = [
        pltpu.make_async_copy(gate_w, wgu.at[0, my_rows], loc.at[1]),
        pltpu.make_async_copy(up_w, wgu.at[1, my_rows], loc.at[2]),
        pltpu.make_async_copy(down_w, wd.at[z], loc.at[3]),
    ]
    for copy in own_w:
        copy.start()

    barrier = pltpu.get_barrier_semaphore()

    def greet(j, _):
        pl.semaphore_signal(barrier, inc=1, device_id=(1 - seg, z, j), device_id_type=MESH)
        return 0

    lax.fori_loop(0, N_ROW, greet, 0)
    for to in (to_yp, to_ym, to_x, to_sib, to_zp, to_zm):
        pl.semaphore_signal(barrier, inc=1, device_id=to, device_id_type=MESH)
    pl.semaphore_wait(barrier, N_ROW + 6)

    def slab(kind, j):
        cols = pl.ds(pl.multiple_of(j * LANES, LANES), LANES)
        src = (
            stream.at[:, :, cols] if kind == 0 else spectrum.at[:, :, cols] if kind == 1 else aux_tx.at[j]
        )
        dst = (rx_stream, rx_spec, aux_rx)[kind].at[me]
        return remote(src, dst, a2a_s.at[kind, j], a2a_r.at[kind, me], (1 - seg, z, j))

    def send_slabs(kind):
        def step(j, _):
            slab(kind, (me + j) % N_ROW).start()
            return 0

        lax.fori_loop(0, N_ROW, step, 0)

    def wait_slabs(kind):
        buf = (rx_stream, rx_spec, aux_rx)[kind]

        def step(j, _):
            remote(buf.at[j], buf.at[j], a2a_s.at[kind, j], a2a_r.at[kind, j], (1 - seg, z, j)).wait_recv()
            return 0

        lax.fori_loop(0, N_ROW, step, 0)

    def w_rows(k):
        return pl.ds(pl.multiple_of(((z + k + 8) % 8) * WROWS, WROWS), WROWS)

    half = (pl.ds(0, WROWS // 2), pl.ds(WROWS // 2, WROWS // 2))

    def ring(step, way, recv):
        sign = -1 if way == 0 else 1
        k = {0: 1, 1: 1, 2: 2, 3: 3, 4: 4, 5: 1, 6: 2, 7: 3, 8: 4}[step]
        k = sign * (k if recv else k - 1)
        if step < 2:
            dst = wgu.at[step, w_rows(k)]
            src = dst if recv else (gate_w, up_w)[step]
        elif step < 4:
            src = dst = wgu.at[:, w_rows(k)]
        elif step == 4:
            src = dst = wgu.at[way, w_rows(k)]
        elif step == 5:
            dst = wd.at[(z + k + 8) % 8]
            src = dst if recv else down_w
        elif step < 8:
            src = dst = wd.at[(z + k + 8) % 8]
        else:
            src = dst = wd.at[(z + k + 8) % 8, half[way]]
        return remote(src, dst, zs.at[way, step], zr.at[way, step], (to_zp, to_zm)[way])

    def ring_send(step):
        for way in (0, 1):
            ring(step, way, False).start()

    def ring_wait(step):
        for way in (0, 1):
            ring(step, way, True).wait_recv()

    send_slabs(0)
    ring_send(0)
    ring_send(1)
    send_slabs(1)

    load_stream.wait()
    rows = FRAMES * BLOCK
    wide = own_stream[...].reshape(rows, D).astype(F32)
    mean_square = jnp.mean(wide * wide, axis=-1, keepdims=True)
    scale = lax.rsqrt(mean_square + 1e-05)
    across = jnp.broadcast_to(scale, (rows, rows)).T
    for j in range(N_ROW):
        aux_tx[j, 0:8, :] = across[0:8, :]
        aux_tx[j, 8:16, :] = jnp.broadcast_to(mixer_gain[:, j * LANES : (j + 1) * LANES], (8, LANES))
    send_slabs(2)

    wait_slabs(0)
    wait_slabs(2)

    def spread(j, _):
        rs_full[j] = jnp.broadcast_to(aux_rx[j, 0:1, :], (rows, rows)).T
        return 0

    lax.fori_loop(0, N_ROW, spread, 0)

    def mixer(f):
        def scale_step(j, _):
            values = rx_stream[j, f].astype(F32)
            factor = rs_full[j, f * BLOCK : (f + 1) * BLOCK, :]
            normed[j] = (values * factor * aux_rx[j, 8:9, :]).astype(BF16)
            return 0

        lax.fori_loop(0, N_ROW, scale_step, 0)
        for j in range(4):
            block = normed[4 * j : 4 * j + 4].reshape(256, LANES)
            col_buf[j] = jnp.dot(t_col[...], block, preferred_element_type=F32).astype(BF16)
        if f == 0:
            wait_slabs(1)
        for kg in range(8):
            pencils = jnp.concatenate([col_buf[j, kg * 64 : (kg + 1) * 64, :] for j in range(4)], axis=0)
            spec = jnp.dot(t_row[...], pencils, preferred_element_type=F32)
            re, im = spec[:128], spec[128:]
            f_re = jnp.concatenate([rx_spec[2 * kg, 0], rx_spec[2 * kg + 1, 0]], axis=0).astype(F32)
            f_im = jnp.concatenate([rx_spec[2 * kg, 1], rx_spec[2 * kg + 1, 1]], axis=0).astype(F32)
            filtered = jnp.concatenate([re * f_re - im * f_im, re * f_im + im * f_re], axis=0)
            back = jnp.dot(t_irow[...], filtered.astype(BF16), preferred_element_type=F32)
            back_buf[kg] = back.astype(BF16)
        for hb in range(8):
            pencils = jnp.concatenate([back_buf[kg, hb * 32 : (hb + 1) * 32, :] for kg in range(8)], axis=0)
            conv = jnp.dot(t_icol[...], pencils, preferred_element_type=F32) * (1.0 / 1024.0)
            values = rx_stream[2 * hb : 2 * hb + 2, f].reshape(128, LANES).astype(F32)
            scaled = normed[2 * hb : 2 * hb + 2].reshape(128, LANES).astype(F32)
            mixed = (values + scaled * conv).astype(BF16)
            full[me, f, hb * BLOCK : (hb + 1) * BLOCK, :] = mixed[:BLOCK]
            full[me, f, 512 + hb * BLOCK : 512 + (hb + 1) * BLOCK, :] = mixed[BLOCK:]

    r = lambda yy, xx: row_of(yy, xx, core)
    xo = 1 - xh
    planes = (pl.ds(0, 512), pl.ds(512, 512))
    routes = [
        (me, None, to_yp, r(ym, xh)),
        (me, None, to_ym, r(yp, xh)),
        (me, None, to_x, r(y, xo)),
        (r(ym, xh), 0, to_yp, r(y2, xh)),
        (r(yp, xh), 1, to_ym, r(y2, xh)),
        (r(y, xo), None, to_yp, r(ym, xo)),
        (r(y, xo), None, to_ym, r(yp, xo)),
        (r(y2, xh), 0, to_x, r(y2, xo)),
        (r(y2, xh), 1, to_x, r(y2, xo)),
    ]
    handed = [
        (me, None), (r(ym, xh), None), (r(yp, xh), None), (r(y, xo), None), (r(y2, xh), 0), (r(y2, xh), 1),
        (r(ym, xo), None), (r(yp, xo), None), (r(y2, xo), 0), (r(y2, xo), 1),
    ]
    flip = lambda slot: slot + 1 - 2 * core
    for slot, plane in handed:
        routes.append((slot, plane, to_sib, flip(slot)))

    def gather(f, m, recv=False):
        sent, plane, to, got = routes[m]
        slot = got if recv else sent
        ref = full.at[slot, f] if plane is None else full.at[slot, f, planes[plane]]
        return remote(ref, ref, ags.at[f, m], agr.at[f, m], to)

    def g_send(f, *ms):
        for m in ms:
            gather(f, m).start()

    def g_wait(f, *ms):
        for m in ms:
            gather(f, m, True).wait_recv()

    def mlp(f, t):
        span = pl.ds(pl.multiple_of(t * 256, 256), 256)
        total = jnp.zeros((256, LANES), F32)
        for j in range(N_ROW):
            v = full[j, f, span, :].astype(F32)
            total = total + v * v
        scale = lax.rsqrt(jnp.sum(total, axis=-1, keepdims=True) * (1.0 / D) + 1e-05)
        for j in range(N_ROW):
            v = full[j, f, span, :].astype(F32)
            gain = mlp_gain[:, j * LANES : (j + 1) * LANES]
            tok[:, j * LANES : (j + 1) * LANES] = (v * scale * gain).astype(BF16)
        gate = jnp.dot(tok[...], wgu[0], preferred_element_type=F32)
        up = jnp.dot(tok[...], wgu[1], preferred_element_type=F32)
        hid[f, span, :] = (gate / (1.0 + jnp.exp(-gate)) * up).astype(BF16)

    mixer(0)
    g_send(0, 0, 1, 2, 9)
    ring_wait(0)
    ring_wait(1)
    for copy in own_w:
        copy.wait()
    ring_send(2)
    ring_send(5)
    mixer(1)
    g_send(1, 0, 1, 2, 9)
    g_wait(0, 0, 1)
    g_send(0, 3, 4, 10, 11)
    g_wait(0, 2)
    g_send(0, 5, 6, 12)
    ring_wait(2)
    ring_send(3)
    ring_wait(5)
    ring_send(6)
    g_wait(0, 3, 4)
    g_send(0, 7, 8, 13, 14)
    g_wait(1, 0, 1)
    g_send(1, 3, 4, 10, 11)
    g_wait(1, 2)
    g_send(1, 5, 6, 12)
    g_wait(0, 5, 6)
    g_send(0, 15, 16)
    ring_wait(3)
    ring_send(4)
    ring_wait(6)
    ring_send(7)
    g_wait(0, 7, 8)
    g_send(0, 17, 18)
    g_wait(1, 3, 4)
    g_send(1, 7, 8, 13, 14)
    g_wait(0, *range(9, 19))
    ring_wait(4)

    def tiles(f, lo, hi):
        def step(t, _):
            mlp(f, t)
            return 0

        lax.fori_loop(lo, hi, step, 0)

    tiles(0, 0, 2)
    g_wait(1, 5, 6)
    g_send(1, 15, 16)
    tiles(0, 2, 4)
    ring_wait(7)
    ring_send(8)
    g_wait(1, 7, 8)
    g_send(1, 17, 18)
    g_wait(1, *range(9, 19))

    q_same = lambda dy: ((y + dy + 4) % 4) * 2 + xh
    q_diff = lambda dy: ((y + dy + 4) % 4) * 2 + xo
    blk = lambda q: pl.ds(pl.multiple_of(q * BLOCK, BLOCK), BLOCK)
    low, high = pl.ds(0, BLOCK // 2), pl.ds(BLOCK // 2, BLOCK // 2)

    def reduce_copy(g, m):
        bufs = [
            (sib_tx.at[g], sib_rx.at[g], to_sib),
            (x1_tx.at[g], x1_rx.at[g], to_x),
            (y2_tx.at[g, 0], y2_rx.at[g, 0], to_yp),
            (y2_tx.at[g, 1], y2_rx.at[g, 1], to_ym),
            (y3_tx.at[g, 0], y3_rx.at[g, 0], to_yp),
            (y3_tx.at[g, 1], y3_rx.at[g, 1], to_ym),
            (x4_tx.at[g], x4_rx.at[g], to_x),
            (y5_tx.at[g, 0], y5_rx.at[g, 0], to_yp),
            (y5_tx.at[g, 1], y5_rx.at[g, 1], to_ym),
        ]
        src, dst, to = bufs[m]
        return remote(src, dst, rss.at[g, m], rsr.at[g, m], to)

    def columns(i):
        return (z - i + 8) % 8, (z + i + 1) % 8

    def stage0(g):
        f, i = g // CHUNKS, g % CHUNKS
        for n, zz in enumerate(columns(i)):
            cols = slice(n * 256, (n + 1) * 256)
            other = hid[f, pl.ds(pl.multiple_of((1 - core) * 512, 512), 512), :]
            sib_tx[g, :, cols] = lax.dot_general(
                other, wd[zz], (((1,), (1,)), ((), ())), preferred_element_type=F32
            ).astype(BF16)
        reduce_copy(g, 0).start()
        for n, zz in enumerate(columns(i)):
            cols = slice(n * 256, (n + 1) * 256)
            mine = hid[f, pl.ds(pl.multiple_of(core * 512, 512), 512), :]
            part[g, :, cols] = lax.dot_general(
                mine, wd[zz], (((1,), (1,)), ((), ())), preferred_element_type=F32
            )

    def stage1(g):
        reduce_copy(g, 0).wait_recv()
        take = lambda q: part[g, blk(q), :] + sib_rx[g, blk(q), :].astype(F32)
        x1_tx[g] = take(q_diff(2)).astype(BF16)
        reduce_copy(g, 1).start()
        y2_tx[g, 0] = take(q_diff(1)).astype(BF16)
        reduce_copy(g, 2).start()
        y2_tx[g, 1] = take(q_diff(-1)).astype(BF16)
        reduce_copy(g, 3).start()
        for q in (q_same(0), q_same(1), q_same(2), q_same(3), q_diff(0)):
            part[g, blk(q), :] = take(q)

    def stage2(g):
        reduce_copy(g, 1).wait_recv()
        total = part[g, blk(q_same(2)), :] + x1_rx[g].astype(F32)
        y3_tx[g, 0] = total[: BLOCK // 2].astype(BF16)
        y3_tx[g, 1] = total[BLOCK // 2 :].astype(BF16)
        reduce_copy(g, 4).start()
        reduce_copy(g, 5).start()
        reduce_copy(g, 2).wait_recv()
        reduce_copy(g, 3).wait_recv()
        total = part[g, blk(q_diff(0)), :] + y2_rx[g, 0].astype(F32) + y2_rx[g, 1].astype(F32)
        x4_tx[g] = total.astype(BF16)
        reduce_copy(g, 6).start()

    def stage3(g):
        reduce_copy(g, 4).wait_recv()
        total = part[g, blk(q_same(1)), :]
        first = total[: BLOCK // 2] + y3_rx[g, 0].astype(F32)
        y5_tx[g, 0] = jnp.concatenate([first, total[BLOCK // 2 :]], axis=0).astype(BF16)
        reduce_copy(g, 7).start()
        reduce_copy(g, 5).wait_recv()
        total = part[g, blk(q_same(3)), :]
        second = total[BLOCK // 2 :] + y3_rx[g, 1].astype(F32)
        y5_tx[g, 1] = jnp.concatenate([total[: BLOCK // 2], second], axis=0).astype(BF16)
        reduce_copy(g, 8).start()

    def stage4(g):
        f, i = g // CHUNKS, g % CHUNKS
        for m in (6, 7, 8):
            reduce_copy(g, m).wait_recv()
        total = part[g, blk(q_same(0)), :] + x4_rx[g].astype(F32)
        total = total + y5_rx[g, 0].astype(F32) + y5_rx[g, 1].astype(F32)
        mine = pl.ds(pl.multiple_of(core * 512 + q_same(0) * BLOCK, BLOCK), BLOCK)
        for n, zz in enumerate(columns(i)):
            got = jnp.concatenate([full[2 * zz, f, mine, :], full[2 * zz + 1, f, mine, :]], axis=1)
            cols = pl.ds(pl.multiple_of(zz * 256, 256), 256)
            out[f, :, cols] = (got.astype(F32) + total[:, n * 256 : (n + 1) * 256]).astype(BF16)

    def step(g, _):
        @pl.when(g == 3)
        def _():
            ring_wait(8)

        @pl.when(g < STEPS)
        def _():
            stage0(g)

        @pl.when((g >= 1) & (g < STEPS + 1))
        def _():
            stage1(g - 1)

        @pl.when((g >= 2) & (g < STEPS + 2))
        def _():
            stage2(g - 2)

        @pl.when((g >= 3) & (g < STEPS + 3))
        def _():
            stage3(g - 3)

        @pl.when(g >= 4)
        def _():
            stage4(g - 4)

        @pl.when(g < CHUNKS)
        def _():
            mlp(1, g)

        return 0

    lax.fori_loop(0, STEPS + 4, step, 0)

    def drain_slabs(j, _):
        for kind in range(3):
            slab(kind, j).wait_send()
        return 0

    lax.fori_loop(0, N_ROW, drain_slabs, 0)
    for way in (0, 1):
        for n in range(9):
            ring(n, way, False).wait_send()
    for f in range(FRAMES):
        for m in range(19):
            gather(f, m).wait_send()

    def drain_reduce(g, _):
        for m in range(9):
            reduce_copy(g, m).wait_send()
        return 0

    lax.fori_loop(0, STEPS, drain_reduce, 0)


def body(stream, mixer_gain, spectrum, mlp_gain, gate_weight, up_weight, down_weight):
    any_spec = pl.BlockSpec(memory_space=pl.ANY)
    vmem_spec = pl.BlockSpec(memory_space=pltpu.VMEM)
    dma = pltpu.SemaphoreType.DMA
    scratch = [
        pltpu.VMEM((FRAMES, BLOCK, D), BF16),
        pltpu.VMEM((N_ROW, FRAMES, BLOCK, LANES), BF16),
        pltpu.VMEM((N_ROW, 2, BLOCK, LANES), BF16),
        pltpu.VMEM((N_ROW, 16, LANES), F32),
        pltpu.VMEM((N_ROW, 16, LANES), F32),
        pltpu.VMEM((N_ROW, LANES, LANES), F32),
        pltpu.VMEM((N_ROW, BLOCK, LANES), BF16),
        pltpu.VMEM((4, 512, LANES), BF16),
        pltpu.VMEM((8, 256, LANES), BF16),
        pltpu.VMEM((N_ROW, FRAMES, TOKENS, LANES), BF16),
        pltpu.VMEM((2, D, HID), BF16),
        pltpu.VMEM((N_Z, WROWS, HID), BF16),
        pltpu.VMEM((256, D), BF16),
        pltpu.VMEM((FRAMES, TOKENS, HID), BF16),
        pltpu.VMEM((STEPS, 512, CCOLS), F32),
        pltpu.VMEM((STEPS, 512, CCOLS), BF16),
        pltpu.VMEM((STEPS, 512, CCOLS), BF16),
        pltpu.VMEM((STEPS, BLOCK, CCOLS), BF16),
        pltpu.VMEM((STEPS, BLOCK, CCOLS), BF16),
        pltpu.VMEM((STEPS, 2, BLOCK, CCOLS), BF16),
        pltpu.VMEM((STEPS, 2, BLOCK, CCOLS), BF16),
        pltpu.VMEM((STEPS, 2, BLOCK // 2, CCOLS), BF16),
        pltpu.VMEM((STEPS, 2, BLOCK // 2, CCOLS), BF16),
        pltpu.VMEM((STEPS, BLOCK, CCOLS), BF16),
        pltpu.VMEM((STEPS, BLOCK, CCOLS), BF16),
        pltpu.VMEM((STEPS, 2, BLOCK, CCOLS), BF16),
        pltpu.VMEM((STEPS, 2, BLOCK, CCOLS), BF16),
        dma((4,)),
        dma((3, N_ROW)),
        dma((3, N_ROW)),
        dma((2, 9)),
        dma((2, 9)),
        dma((FRAMES, 19)),
        dma((FRAMES, 19)),
        dma((STEPS, 9)),
        dma((STEPS, 9)),
    ]
    result = pl.pallas_call(
        kernel,
        out_shape=jax.ShapeDtypeStruct((FRAMES, BLOCK, D), BF16),
        in_specs=[any_spec, vmem_spec, any_spec, vmem_spec, any_spec, any_spec, any_spec] + [vmem_spec] * 4,
        out_specs=vmem_spec,
        scratch_shapes=scratch,
        compiler_params=pltpu.CompilerParams(
            collective_id=0, has_side_effects=True, vmem_limit_bytes=62 * 2**20
        ),
        cost_estimate=pl.CostEstimate(flops=14_000_000_000, bytes_accessed=6 * 2**20, transcendentals=2**20),
    )(
        stream.reshape(FRAMES, BLOCK, D),
        mixer_gain,
        spectrum.reshape(2, BLOCK, D),
        mlp_gain,
        gate_weight[0],
        up_weight[0],
        down_weight[0],
        *tables(),
    )
    return result.reshape(stream.shape)


def solution(mesh):
    return jax.shard_map(
        body,
        mesh=mesh,
        in_specs=(
            P("segment", "frame", "row", None, None),
            P("segment", None),
            P("segment", None, "row", None, None),
            P("segment", None),
            P("segment", "frame", "row"),
            P("segment", "frame", "row"),
            P("segment", "frame", "row"),
        ),
        out_specs=P("segment", "frame", "row", None, None),
        check_vma=False,
    )
```

time: 407 us -> 125 us (0.31)
  waiting for transfers between devices: 326 us -> 0 us
  Pallas kernels: 0 us -> 123 us
  matrix products: 32.9 us -> 0 us
  starting transfers between devices: 13.6 us -> 0 us
  between operations: 13.3 us -> 0.01 us
  local copies, waits for them, and re-layouts: 15.1 us -> 1.88 us
  other arithmetic: 5.24 us -> 0 us
    all_gather x4 -> x0, waiting for transfers between devices: 167 us -> none  [the longest x1 76.5 us: body(): lax.all_gather(jnp.swapaxes(normed_next, 0, 1), 'row', axis=0, tiled=True)]
    pallas_call x0 -> x1, Pallas kernels: none -> 123 us  [body(): pl.pallas_call(kernel, out_shape=jax.ShapeDtypeStruct((FRAMES, BLOCK, D),...]
    reduce_scatter x1 -> x0, waiting for transfers between devices: 112 us -> none  [body(): lax.psum_scatter(lax.dot_general(hidden, down_full, (((1,), (1,)), ((), (...]
    all_to_all x2 -> x0, waiting for transfers between devices: 34 us -> none  [the longest x1 17.1 us: body(): lax.all_to_all(back, 'row', split_axis=2, concat_axis=3, tiled=True)]
    dot_general x7 -> x0, matrix products: 32.9 us -> none  [the longest x1 10.5 us: body(): gate = jnp.dot(flat_tokens, gate_full, preferred_element_type=jnp.float32)]
    all_to_all x2 -> x0, starting transfers between devices: 12.8 us -> none  [the longest x1 8.45 us: body(): lax.all_to_all(col_spec, 'row', split_axis=3, concat_axis=1, tiled=True)]
    ppermute x1 -> x0, waiting for transfers between devices: 12.1 us -> none  [from_behind(): lax.ppermute(value, axis, [(i, (i + by) % devices) for i in range(devices)])]
    all_gather x1 -> x0, local copies, waits for them, and re-layouts: 8.28 us -> none  [body(): lax.all_gather(jnp.swapaxes(normed_next, 0, 1), 'row', axis=0, tiled=True)]
  transfers between devices with their start and end apart: 8 -> 0, of which waited for: 8 -> 0; matrix products, arithmetic and copies ran while one was open for 7% -> 0% of each run, Pallas kernels for 0% -> 0%
where the time goes in v1:
time: 125 us
  Pallas kernels  123 us (98%)
  local copies, waits for them, and re-layouts  1.88 us (2%)
    pallas_call x1, Pallas kernels, body(): pl.pallas_call(kernel, out_shape=jax.ShapeDtypeStruct((FRAMES, BLOCK, D),...  123 us

profile of v1, /device:TPU:1, one launch (start us, length us, event | category | flops | bytes accessed | tf_op | source)
XLA Modules:
  0.0 125.3 jit_solution(14587065864582469059)
XLA Ops:
  0.0 123.4 %shard_map.109 = bf16[2,64,2048]{2,1,0:T(8,128)(2,1)} custom-call(bf16[2,64,2048]{2,1,0:T(8,128)(2,1)} %bitcast.7, f32[1,2048]{1,0:T(1,128)} %mixer_gain.1, bf16[2,64,2048]{2,1,0:T(8,128)(2,1)} %bitcast.8, f32[1,2048]{1,0:T(1,128)} %mlp_gain.1, bf16[256,512]{1,0:T(8,128)(2,1)} %bitcast.9, bf16[256,512]{1,0:T(8,128)(2,1)} %bitcast.10, ...), custom_call_target="tpu_custom_call" | custom-call | flops 14000000000 | bytes 6291456 | tf_op jit(solution)/shard_map/pallas_call | solution.py:494
  123.4 1.9 %copy.13 = bf16[1,2,2,32,2048]{4,3,2,1,0:T(8,128)(2,1)} copy(bf16[1,2,2,32,2048]{4,3,2,1,0:T(8,128)(2,1)} %bitcast.6) | data formatting | bytes 1048576

commit v2 on v1

v2 whole, which is shorter than its diff:
```python
import functools
import math

import jax
import jax.numpy as jnp
import numpy as np
from jax import lax
from jax.experimental import pallas as pl
from jax.experimental.pallas import tpu as pltpu
from jax.sharding import PartitionSpec as P

MESH = pl.DeviceIdType.MESH
BF16, F32 = jnp.bfloat16, jnp.float32

N_ROW, N_Y, N_Z = 16, 4, 8
FRAMES = 2
BLOCK = 64
TOKENS = N_ROW * BLOCK
LANES = 128
D, HID, WROWS = 2048, 512, 256
OWN = 3
STEPS = FRAMES * N_Z
CCOLS = D // N_Z
LAGS = (1, 4, 7, 10)
LIVE = LAGS[-1] + 1


def tables():
    n = 32
    index = np.arange(n)
    angle = (index[:, None] * index[None, :] % n) * (2.0 * math.pi / n)
    cos, sin = np.cos(angle), np.sin(angle)
    cos[np.abs(cos) < 1e-9] = 0.0
    sin[np.abs(sin) < 1e-9] = 0.0
    eye4, eye8 = np.eye(4), np.eye(8)
    fwd = np.stack((cos, -sin))
    col = np.einsum("cwk,hg->kchgw", fwd, eye8).reshape(512, 256)
    mix = np.empty((2, 2, n, n))
    mix[0, 0], mix[0, 1], mix[1, 0], mix[1, 1] = cos, -sin, sin, cos
    row = np.einsum("cejhm,kl->ekmjlch", mix.reshape(2, 2, 4, 8, n), eye4).reshape(256, 256)
    inv = np.empty((2, 2, n, n))
    inv[0, 0], inv[0, 1], inv[1, 0], inv[1, 1] = cos, sin, -sin, cos
    irow = np.einsum("cemah,kl->ahkeclm", inv.reshape(2, 2, n, 8, 4), eye4).reshape(256, 256)
    icol = np.einsum("eakw,hg->hwagke", fwd.reshape(2, 8, 4, n), eye4).reshape(128, 256)
    return jnp.asarray(np.concatenate((col, row, irow, icol)), BF16)


def kernel(
    stream, mixer_gain, spectrum, mlp_gain, gate_w, up_w, down_w,
    tables_ref,
    out,
    table, own_stream, rx_stream, rx_spec, aux_tx, aux_rx, rs_full, normed, col_buf, spec_buf, back_buf,
    full, wgu, wd, tok, tok_last, acc, hid,
    part, sib_tx, sib_rx,
    x1_tx, x1_rx, y2_tx, y2_rx, y3_tx, y3_rx, x4_tx, x4_rx, y5_tx, y5_rx,
    loc, a2a_s, a2a_r, spec_s, spec_r, zs, zr, ags, agr, rss, rsr,
):
    seg, z, me = lax.axis_index("segment"), lax.axis_index("frame"), lax.axis_index("row")
    core, xh, y = me % 2, (me // 2) % 2, me // 4
    row_of = lambda yy, xx, cc: (yy * 2 + xx) * 2 + cc
    ym, yp, y2 = (y + 3) % 4, (y + 1) % 4, (y + 2) % 4
    zm, zp = (z + 7) % 8, (z + 1) % 8
    to_yp, to_ym = (seg, z, row_of(yp, xh, core)), (seg, z, row_of(ym, xh, core))
    to_x, to_sib = (seg, z, row_of(y, 1 - xh, core)), (seg, z, row_of(y, xh, 1 - core))
    to_zp, to_zm = (seg, zp, me), (seg, zm, me)

    def remote(src, dst, ssem, rsem, to):
        return pltpu.make_async_remote_copy(
            src_ref=src, dst_ref=dst, send_sem=ssem, recv_sem=rsem, device_id=to, device_id_type=MESH
        )

    load_stream = pltpu.make_async_copy(stream, own_stream, loc.at[0])
    load_stream.start()
    load_table = pltpu.make_async_copy(tables_ref, table, loc.at[4])
    load_table.start()
    own_w = [
        pltpu.make_async_copy(gate_w, wgu.at[0, OWN], loc.at[1]),
        pltpu.make_async_copy(up_w, wgu.at[1, OWN], loc.at[2]),
        pltpu.make_async_copy(down_w, wd.at[OWN], loc.at[3]),
    ]
    for copy in own_w:
        copy.start()

    t_col, t_row, t_irow, t_icol = (table.at[a:b] for a, b in ((0, 512), (512, 768), (768, 1024), (1024, 1152)))

    barrier = pltpu.get_barrier_semaphore()

    def greet(j, _):
        pl.semaphore_signal(barrier, inc=1, device_id=(1 - seg, z, j), device_id_type=MESH)
        return 0

    lax.fori_loop(0, N_ROW, greet, 0)
    for to in (to_yp, to_ym, to_x, to_sib, to_zp, to_zm):
        pl.semaphore_signal(barrier, inc=1, device_id=to, device_id_type=MESH)
    pl.semaphore_wait(barrier, N_ROW + 6)

    def landing(kind, j):
        if kind < 2:
            return rx_stream.at[j, kind]
        return aux_rx.at[j] if kind == 2 else rx_spec.at[j, z % 2]

    def slab(kind, j):
        cols = pl.ds(pl.multiple_of(j * LANES, LANES), LANES)
        if kind < 2:
            src = stream.at[kind, :, cols]
        else:
            src = aux_tx.at[j] if kind == 2 else spectrum.at[z % 2, :, cols]
        return remote(src, landing(kind, me), a2a_s.at[kind, j], a2a_r.at[kind, me], (1 - seg, z, j))

    def send_slabs(kind):
        def step(j, _):
            slab(kind, (me + j) % N_ROW).start()
            return 0

        lax.fori_loop(0, N_ROW, step, 0)

    def wait_slabs(kind):
        def step(j, _):
            ref = landing(kind, j)
            remote(ref, ref, a2a_s.at[kind, j], a2a_r.at[kind, j], (1 - seg, z, j)).wait_recv()
            return 0

        lax.fori_loop(0, N_ROW, step, 0)

    def other_part(m, recv=False):
        to, slots = ((to_zp, pl.ds(0, N_ROW // 2)), (to_zm, pl.ds(N_ROW // 2, N_ROW // 2)))[m]
        ref = rx_spec.at[slots, (z + 1) % 2 if recv else z % 2]
        return remote(ref, ref, spec_s.at[m], spec_r.at[m], to)

    half = (pl.ds(0, WROWS // 2), pl.ds(WROWS // 2, WROWS // 2))

    def ring(step, way):
        k = step // 2 + 1 if step < 6 else 4 if step == 6 else step - 6
        sign = -1 if way == 0 else 1
        was, now = OWN + sign * (k - 1), (OWN + sign * k) % N_Z
        if step < 7:
            n = step % 2 if step < 6 else way
            dst = wgu.at[n, now]
            src = wgu.at[n, was] if step > 1 else (gate_w, up_w)[n]
        elif step < 10:
            dst = wd.at[now]
            src = wd.at[was] if step > 7 else down_w
        else:
            src, dst = wd.at[was, half[way]], wd.at[now, half[way]]
        return remote(src, dst, zs.at[way, step], zr.at[way, step], (to_zp, to_zm)[way])

    def ring_send(step):
        for way in (0, 1):
            ring(step, way).start()

    def ring_wait(step):
        for way in (0, 1):
            ring(step, way).wait_recv()

    send_slabs(3)
    send_slabs(0)
    ring_send(0)

    load_stream.wait()
    rows = FRAMES * BLOCK
    wide = own_stream[...].reshape(rows, D).astype(F32)
    mean_square = jnp.mean(wide * wide, axis=-1, keepdims=True)
    scale = lax.rsqrt(mean_square + 1e-05)
    across = jnp.broadcast_to(scale, (rows, rows)).T
    for j in range(N_ROW):
        aux_tx[j, 0:4, :] = across[0:4, :]
        aux_tx[j, 4:8, :] = jnp.broadcast_to(mixer_gain[:, j * LANES : (j + 1) * LANES], (4, LANES))
    send_slabs(2)
    send_slabs(1)
    wait_slabs(3)
    for m in range(2):
        other_part(m).start()
    ring_send(1)

    wait_slabs(0)
    wait_slabs(2)

    def spread(j, _):
        rs_full[j] = jnp.broadcast_to(aux_rx[j, 0:1, :], (rows, rows)).T
        return 0

    lax.fori_loop(0, N_ROW, spread, 0)

    def mixer_columns(f):
        def scale_step(j, _):
            values = rx_stream[j, f].astype(F32)
            factor = rs_full[j, f * BLOCK : (f + 1) * BLOCK, :]
            normed[f, j] = (values * factor * aux_rx[j, 4:5, :]).astype(BF16)
            return 0

        lax.fori_loop(0, N_ROW, scale_step, 0)
        for j in range(4):
            block = normed[f, 4 * j : 4 * j + 4].reshape(256, LANES)
            col_buf[f, j] = jnp.dot(t_col[...], block, preferred_element_type=F32).astype(BF16)

    def mixer_rows(f):
        for kg in range(8):
            pencils = jnp.concatenate([col_buf[f, j, kg * 64 : (kg + 1) * 64, :] for j in range(4)], axis=0)
            spec_buf[f, kg] = jnp.dot(t_row[...], pencils, preferred_element_type=F32)

    def mixer_filter(f):
        for kg in range(8):
            re, im = spec_buf[f, kg, :128], spec_buf[f, kg, 128:]
            f_re = jnp.concatenate([rx_spec[2 * kg, 0], rx_spec[2 * kg + 1, 0]], axis=0).astype(F32)
            f_im = jnp.concatenate([rx_spec[2 * kg, 1], rx_spec[2 * kg + 1, 1]], axis=0).astype(F32)
            filtered = jnp.concatenate([re * f_re - im * f_im, re * f_im + im * f_re], axis=0)
            back = jnp.dot(t_irow[...], filtered.astype(BF16), preferred_element_type=F32)
            back_buf[kg] = back.astype(BF16)
        for hb in range(8):
            pencils = jnp.concatenate([back_buf[kg, hb * 32 : (hb + 1) * 32, :] for kg in range(8)], axis=0)
            conv = jnp.dot(t_icol[...], pencils, preferred_element_type=F32) * (1.0 / 1024.0)
            values = rx_stream[2 * hb : 2 * hb + 2, f].reshape(128, LANES).astype(F32)
            scaled = normed[f, 2 * hb : 2 * hb + 2].reshape(128, LANES).astype(F32)
            mixed = (values + scaled * conv).astype(BF16)
            full[me, f, hb * BLOCK : (hb + 1) * BLOCK, :] = mixed[:BLOCK]
            full[me, f, 512 + hb * BLOCK : 512 + (hb + 1) * BLOCK, :] = mixed[BLOCK:]

    r = lambda yy, xx: row_of(yy, xx, core)
    xo = 1 - xh
    planes = (pl.ds(0, 512), pl.ds(512, 512))
    routes = [
        (me, None, to_yp, r(ym, xh)),
        (me, None, to_ym, r(yp, xh)),
        (me, None, to_x, r(y, xo)),
        (r(ym, xh), 0, to_yp, r(y2, xh)),
        (r(yp, xh), 1, to_ym, r(y2, xh)),
        (r(y, xo), None, to_yp, r(ym, xo)),
        (r(y, xo), None, to_ym, r(yp, xo)),
        (r(y2, xh), 0, to_x, r(y2, xo)),
        (r(y2, xh), 1, to_x, r(y2, xo)),
    ]
    handed = [
        (me, None), (r(ym, xh), None), (r(yp, xh), None), (r(y, xo), None), (r(y2, xh), 0), (r(y2, xh), 1),
        (r(ym, xo), None), (r(yp, xo), None), (r(y2, xo), 0), (r(y2, xo), 1),
    ]
    flip = lambda slot: slot + 1 - 2 * core
    for slot, plane in handed:
        routes.append((slot, plane, to_sib, flip(slot)))

    def gather(f, m, recv=False):
        sent, plane, to, got = routes[m]
        slot = got if recv else sent
        ref = full.at[slot, f] if plane is None else full.at[slot, f, planes[plane]]
        return remote(ref, ref, ags.at[f, m], agr.at[f, m], to)

    def g_send(f, *ms):
        for m in ms:
            gather(f, m).start()

    def g_wait(f, *ms):
        for m in ms:
            gather(f, m, True).wait_recv()

    most = (N_Z - 1) * WROWS

    def mlp_most(f, t):
        span = pl.ds(pl.multiple_of(t * 256, 256), 256)
        total = jnp.zeros((256, LANES), F32)
        for j in range(N_ROW):
            v = full[j, f, span, :].astype(F32)
            total = total + v * v
        scale = lax.rsqrt(jnp.sum(total, axis=-1, keepdims=True) * (1.0 / D) + 1e-05)
        for slot in range(N_Z):
            zz = (z + slot + N_Z - OWN) % N_Z
            for n in range(2):
                v = full[2 * zz + n, f, span, :].astype(F32)
                gain = mlp_gain[:, pl.ds(pl.multiple_of((2 * zz + n) * LANES, LANES), LANES)]
                v = (v * scale * gain).astype(BF16)
                if slot < N_Z - 1:
                    tok[:, slot * 256 + n * LANES : slot * 256 + (n + 1) * LANES] = v
                else:
                    tok_last[f, span, n * LANES : (n + 1) * LANES] = v
        for n in range(2):
            weight = wgu[n, : N_Z - 1].reshape(most, HID)
            acc[n, f, span, :] = jnp.dot(tok[...], weight, preferred_element_type=F32)

    def mlp_rest(f, t):
        span = pl.ds(pl.multiple_of(t * 256, 256), 256)
        last = tok_last[f, span, :]
        gate = acc[0, f, span, :] + jnp.dot(last, wgu[0, N_Z - 1], preferred_element_type=F32)
        up = acc[1, f, span, :] + jnp.dot(last, wgu[1, N_Z - 1], preferred_element_type=F32)
        hid[f, span, :] = (gate / (1.0 + jnp.exp(-gate)) * up).astype(BF16)

    load_table.wait()
    mixer_columns(0)
    mixer_rows(0)
    for m in range(2):
        other_part(m, True).wait_recv()
    for copy in own_w:
        copy.wait()
    mixer_filter(0)
    g_send(0, 0, 1, 2, 9)
    ring_wait(0)
    ring_send(2)
    wait_slabs(1)
    mixer_columns(1)
    mixer_rows(1)
    mixer_filter(1)
    g_send(1, 0, 1, 2, 9)
    ring_wait(1)
    ring_send(3)
    g_wait(0, 0, 1)
    g_send(0, 3, 4, 10, 11)
    g_wait(0, 2)
    g_send(0, 5, 6, 12)
    ring_wait(2)
    ring_send(4)
    g_wait(1, 0, 1)
    g_send(1, 3, 4, 10, 11)
    g_wait(1, 2)
    g_send(1, 5, 6, 12)
    ring_wait(3)
    ring_send(5)
    g_wait(0, 3, 4)
    g_send(0, 7, 8, 13, 14)
    g_wait(0, 5, 6)
    g_send(0, 15, 16)
    ring_wait(4)
    ring_wait(5)
    ring_send(6)
    ring_send(7)
    g_wait(1, 3, 4)
    g_send(1, 7, 8, 13, 14)
    g_wait(0, 7, 8)
    g_send(0, 17, 18)
    g_wait(0, *range(9, 19))

    def tiles(part_of, f, lo, hi):
        def step(t, _):
            part_of(f, t)
            return 0

        lax.fori_loop(lo, hi, step, 0)

    tiles(mlp_most, 0, 0, 2)
    g_wait(1, 5, 6)
    g_send(1, 15, 16)
    tiles(mlp_most, 0, 2, 4)
    g_wait(1, 7, 8)
    g_send(1, 17, 18)
    ring_wait(6)
    tiles(mlp_rest, 0, 0, 4)
    ring_wait(7)
    ring_send(8)

    q_same = lambda dy: ((y + dy + 4) % 4) * 2 + xh
    q_diff = lambda dy: ((y + dy + 4) % 4) * 2 + xo
    blk = lambda q: pl.ds(pl.multiple_of(q * BLOCK, BLOCK), BLOCK)
    low, high = pl.ds(0, BLOCK // 2), pl.ds(BLOCK // 2, BLOCK // 2)

    def reduce_copy(g, m):
        bufs = [
            (sib_tx.at[g], sib_rx.at[g], to_sib),
            (x1_tx.at[g], x1_rx.at[g], to_x),
            (y2_tx.at[g, 0], y2_rx.at[g, 0], to_yp),
            (y2_tx.at[g, 1], y2_rx.at[g, 1], to_ym),
            (y3_tx.at[g, 0], y3_rx.at[g, 0], to_yp),
            (y3_tx.at[g, 1], y3_rx.at[g, 1], to_ym),
            (x4_tx.at[g], x4_rx.at[g], to_x),
            (y5_tx.at[g, 0], y5_rx.at[g, 0], to_yp),
            (y5_tx.at[g, 1], y5_rx.at[g, 1], to_ym),
        ]
        src, dst, to = bufs[m]
        return remote(src, dst, rss.at[g, m], rsr.at[g, m], to)

    def place(g):
        late = g - 6
        f = jnp.where(g < 6, g // 3, jnp.where(g < 14, late // 2 % 2, g - 14))
        n = jnp.where(g < 6, g % 3, jnp.where(g < 14, 3 + late // 4 * 2 + late % 2, 7))
        return f, (n + 1) // 2 * (n % 2 * 2 - 1)

    def stage0(g):
        f, off = place(g)
        weight = wd[OWN + off]
        dims = (((1,), (1,)), ((), ()))
        other = hid[f, pl.ds(pl.multiple_of((1 - core) * 512, 512), 512), :]
        sib_tx[g] = lax.dot_general(other, weight, dims, preferred_element_type=F32).astype(BF16)
        reduce_copy(g, 0).start()
        mine = hid[f, pl.ds(pl.multiple_of(core * 512, 512), 512), :]
        part[g % LIVE] = lax.dot_general(mine, weight, dims, preferred_element_type=F32)

    def stage1(g):
        reduce_copy(g, 0).wait_recv()
        take = lambda q: part[g % LIVE, blk(q), :] + sib_rx[g, blk(q), :].astype(F32)
        x1_tx[g] = take(q_diff(2)).astype(BF16)
        reduce_copy(g, 1).start()
        y2_tx[g, 0] = take(q_diff(1)).astype(BF16)
        reduce_copy(g, 2).start()
        y2_tx[g, 1] = take(q_diff(-1)).astype(BF16)
        reduce_copy(g, 3).start()
        for q in (q_same(0), q_same(1), q_same(2), q_same(3), q_diff(0)):
            part[g % LIVE, blk(q), :] = take(q)

    def stage2(g):
        reduce_copy(g, 1).wait_recv()
        total = part[g % LIVE, blk(q_same(2)), :] + x1_rx[g].astype(F32)
        y3_tx[g, 0] = total[: BLOCK // 2].astype(BF16)
        y3_tx[g, 1] = total[BLOCK // 2 :].astype(BF16)
        reduce_copy(g, 4).start()
        reduce_copy(g, 5).start()
        reduce_copy(g, 2).wait_recv()
        reduce_copy(g, 3).wait_recv()
        total = part[g % LIVE, blk(q_diff(0)), :] + y2_rx[g, 0].astype(F32) + y2_rx[g, 1].astype(F32)
        x4_tx[g] = total.astype(BF16)
        reduce_copy(g, 6).start()

    def stage3(g):
        reduce_copy(g, 4).wait_recv()
        total = part[g % LIVE, blk(q_same(1)), :]
        first = total[: BLOCK // 2] + y3_rx[g, 0].astype(F32)
        y5_tx[g, 0] = jnp.concatenate([first, total[BLOCK // 2 :]], axis=0).astype(BF16)
        reduce_copy(g, 7).start()
        reduce_copy(g, 5).wait_recv()
        total = part[g % LIVE, blk(q_same(3)), :]
        second = total[BLOCK // 2 :] + y3_rx[g, 1].astype(F32)
        y5_tx[g, 1] = jnp.concatenate([total[: BLOCK // 2], second], axis=0).astype(BF16)
        reduce_copy(g, 8).start()

    def stage4(g):
        f, off = place(g)
        zz = (z + off + N_Z) % N_Z
        for m in (6, 7, 8):
            reduce_copy(g, m).wait_recv()
        total = part[g % LIVE, blk(q_same(0)), :] + x4_rx[g].astype(F32)
        total = total + y5_rx[g, 0].astype(F32) + y5_rx[g, 1].astype(F32)
        mine = pl.ds(pl.multiple_of(core * 512 + q_same(0) * BLOCK, BLOCK), BLOCK)
        got = jnp.concatenate([full[2 * zz, f, mine, :], full[2 * zz + 1, f, mine, :]], axis=1)
        cols = pl.ds(pl.multiple_of(zz * 256, 256), 256)
        out[f, :, cols] = (got.astype(F32) + total).astype(BF16)

    def step(g, _):
        for n, when in enumerate((4, 9)):

            @pl.when(g == when)
            def _(n=n):
                ring_wait(8 + n)
                ring_send(9 + n)

        @pl.when(g == 14)
        def _():
            ring_wait(10)

        @pl.when(g < STEPS)
        def _():
            stage0(g)

        for lag, stage in zip(LAGS, (stage1, stage2, stage3, stage4)):

            @pl.when((g >= lag) & (g < STEPS + lag))
            def _(lag=lag, stage=stage):
                stage(g - lag)

        @pl.when(g == 0)
        def _():
            g_wait(1, *range(9, 19))
            tiles(mlp_most, 1, 0, 2)

        @pl.when(g == 1)
        def _():
            tiles(mlp_most, 1, 2, 3)

        @pl.when(g == 2)
        def _():
            tiles(mlp_most, 1, 3, 4)
            tiles(mlp_rest, 1, 0, 4)

        return 0

    lax.fori_loop(0, STEPS + LAGS[-1], step, 0)

    def drain_slabs(j, _):
        for kind in range(4):
            slab(kind, j).wait_send()
        return 0

    lax.fori_loop(0, N_ROW, drain_slabs, 0)
    for m in range(2):
        other_part(m).wait_send()
    for way in (0, 1):
        for n in range(11):
            ring(n, way).wait_send()
    for f in range(FRAMES):
        for m in range(19):
            gather(f, m).wait_send()

    def drain_reduce(g, _):
        for m in range(9):
            reduce_copy(g, m).wait_send()
        return 0

    lax.fori_loop(0, STEPS, drain_reduce, 0)


def body(stream, mixer_gain, spectrum, mlp_gain, gate_weight, up_weight, down_weight):
    any_spec = pl.BlockSpec(memory_space=pl.ANY)
    vmem_spec = pl.BlockSpec(memory_space=pltpu.VMEM)
    dma = pltpu.SemaphoreType.DMA
    scratch = [
        pltpu.VMEM((1152, 256), BF16),
        pltpu.VMEM((FRAMES, BLOCK, D), BF16),
        pltpu.VMEM((N_ROW, FRAMES, BLOCK, LANES), BF16),
        pltpu.VMEM((N_ROW, 2, BLOCK, LANES), BF16),
        pltpu.VMEM((N_ROW, 8, LANES), F32),
        pltpu.VMEM((N_ROW, 8, LANES), F32),
        pltpu.VMEM((N_ROW, LANES, LANES), F32),
        pltpu.VMEM((FRAMES, N_ROW, BLOCK, LANES), BF16),
        pltpu.VMEM((FRAMES, 4, 512, LANES), BF16),
        pltpu.VMEM((FRAMES, 8, 256, LANES), F32),
        pltpu.VMEM((8, 256, LANES), BF16),
        pltpu.VMEM((N_ROW, FRAMES, TOKENS, LANES), BF16),
        pltpu.VMEM((2, N_Z, WROWS, HID), BF16),
        pltpu.VMEM((N_Z, WROWS, HID), BF16),
        pltpu.VMEM((256, D - WROWS), BF16),
        pltpu.VMEM((FRAMES, TOKENS, WROWS), BF16),
        pltpu.VMEM((2, FRAMES, TOKENS, HID), F32),
        pltpu.VMEM((FRAMES, TOKENS, HID), BF16),
        pltpu.VMEM((LIVE, 512, CCOLS), F32),
        pltpu.VMEM((STEPS, 512, CCOLS), BF16),
        pltpu.VMEM((STEPS, 512, CCOLS), BF16),
        pltpu.VMEM((STEPS, BLOCK, CCOLS), BF16),
        pltpu.VMEM((STEPS, BLOCK, CCOLS), BF16),
        pltpu.VMEM((STEPS, 2, BLOCK, CCOLS), BF16),
        pltpu.VMEM((STEPS, 2, BLOCK, CCOLS), BF16),
        pltpu.VMEM((STEPS, 2, BLOCK // 2, CCOLS), BF16),
        pltpu.VMEM((STEPS, 2, BLOCK // 2, CCOLS), BF16),
        pltpu.VMEM((STEPS, BLOCK, CCOLS), BF16),
        pltpu.VMEM((STEPS, BLOCK, CCOLS), BF16),
        pltpu.VMEM((STEPS, 2, BLOCK, CCOLS), BF16),
        pltpu.VMEM((STEPS, 2, BLOCK, CCOLS), BF16),
        dma((5,)),
        dma((4, N_ROW)),
        dma((4, N_ROW)),
        dma((2,)),
        dma((2,)),
        dma((2, 11)),
        dma((2, 11)),
        dma((FRAMES, 19)),
        dma((FRAMES, 19)),
        dma((STEPS, 9)),
        dma((STEPS, 9)),
    ]
    result = pl.pallas_call(
        kernel,
        out_shape=jax.ShapeDtypeStruct((FRAMES, BLOCK, D), BF16),
        in_specs=[any_spec, vmem_spec, any_spec, vmem_spec] + [any_spec] * 4,
        out_specs=vmem_spec,
        scratch_shapes=scratch,
        compiler_params=pltpu.CompilerParams(
            collective_id=0, has_side_effects=True, vmem_limit_bytes=62 * 2**20
        ),
        cost_estimate=pl.CostEstimate(flops=14_000_000_000, bytes_accessed=6 * 2**20, transcendentals=2**20),
    )(
        stream.reshape(FRAMES, BLOCK, D),
        mixer_gain,
        spectrum.reshape(2, BLOCK, D),
        mlp_gain,
        gate_weight[0],
        up_weight[0],
        down_weight[0],
        tables(),
    )
    return result.reshape(stream.shape)


def solution(mesh):
    return jax.shard_map(
        body,
        mesh=mesh,
        in_specs=(
            P("segment", "frame", "row", None, None),
            P("segment", None),
            P("segment", None, "row", None, None),
            P("segment", None),
            P("segment", "frame", "row"),
            P("segment", "frame", "row"),
            P("segment", "frame", "row"),
        ),
        out_specs=P("segment", "frame", "row", None, None),
        check_vma=False,
    )
```

time: 125 us -> 113 us (0.904); the launches traced: 125 us -> 112 us
  Pallas kernels: 123 us -> 110 us
    pallas_call x1, Pallas kernels: 123 us -> 110 us  [body(): pl.pallas_call(kernel, out_shape=jax.ShapeDtypeStruct((FRAMES, BLOCK, D),...]
where the time goes in v2:
time: 113 us; the launch traced here: 112 us
  Pallas kernels  110 us (97%)
  local copies, waits for them, and re-layouts  1.88 us (2%)
    pallas_call x1, Pallas kernels, body(): pl.pallas_call(kernel, out_shape=jax.ShapeDtypeStruct((FRAMES, BLOCK, D),...  110 us

profile of v2, /device:TPU:1, one launch (start us, length us, event | category | flops | bytes accessed | tf_op | source)
XLA Modules:
  0.0 111.9 jit_solution(942324448927148210)
XLA Ops:
  0.0 110.1 %shard_map.82 = bf16[2,64,2048]{2,1,0:T(8,128)(2,1)} custom-call(bf16[2,64,2048]{2,1,0:T(8,128)(2,1)} %bitcast.7, f32[1,2048]{1,0:T(1,128)} %mixer_gain.1, bf16[2,64,2048]{2,1,0:T(8,128)(2,1)} %bitcast.8, f32[1,2048]{1,0:T(1,128)} %mlp_gain.1, bf16[256,512]{1,0:T(8,128)(2,1)} %bitcast.9, bf16[256,512]{1,0:T(8,128)(2,1)} %bitcast.10, ...), custom_call_target="tpu_custom_call" | custom-call | flops 14000000000 | bytes 6291456 | tf_op jit(solution)/shard_map/pallas_call | solution.py:542
  110.1 1.9 %copy.10 = bf16[1,2,2,32,2048]{4,3,2,1,0:T(8,128)(2,1)} copy(bf16[1,2,2,32,2048]{4,3,2,1,0:T(8,128)(2,1)} %bitcast.6) | data formatting | bytes 1048576

commit v3 on v2

--- a/solution.py
+++ b/solution.py
@@ -46,14 +46,14 @@
 
 
 def kernel(
-    stream, mixer_gain, spectrum, mlp_gain, gate_w, up_w, down_w,
+    stream, mixer_gain_ref, spectrum, mlp_gain_ref, gate_w, up_w, down_w,
     tables_ref,
-    out,
-    table, own_stream, rx_stream, rx_spec, aux_tx, aux_rx, rs_full, normed, col_buf, spec_buf, back_buf,
-    full, wgu, wd, tok, tok_last, acc, hid,
+    out_ref,
+    out, table, mixer_gain, mlp_gain, own_stream, rx_stream, rx_spec, aux_tx, aux_rx, rs_full, normed, col_buf, spec_buf, back_buf,
+    full, wgu, wd, gain_col, folded, scales, acc, hid,
     part, sib_tx, sib_rx,
     x1_tx, x1_rx, y2_tx, y2_rx, y3_tx, y3_rx, x4_tx, x4_rx, y5_tx, y5_rx,
-    loc, a2a_s, a2a_r, spec_s, spec_r, zs, zr, ags, agr, rss, rsr,
+    loc, outs, a2a_s, a2a_r, spec_s, spec_r, zs, zr, ags, agr, rss, rsr,
 ):
     seg, z, me = lax.axis_index("segment"), lax.axis_index("frame"), lax.axis_index("row")
     core, xh, y = me % 2, (me // 2) % 2, me // 4
@@ -73,6 +73,12 @@
     load_stream.start()
     load_table = pltpu.make_async_copy(tables_ref, table, loc.at[4])
     load_table.start()
+    load_gains = [
+        pltpu.make_async_copy(mixer_gain_ref, mixer_gain, loc.at[5]),
+        pltpu.make_async_copy(mlp_gain_ref, mlp_gain, loc.at[6]),
+    ]
+    for copy in load_gains:
+        copy.start()
     own_w = [
         pltpu.make_async_copy(gate_w, wgu.at[0, OWN], loc.at[1]),
         pltpu.make_async_copy(up_w, wgu.at[1, OWN], loc.at[2]),
@@ -144,8 +150,8 @@
             src, dst = wd.at[was, half[way]], wd.at[now, half[way]]
         return remote(src, dst, zs.at[way, step], zr.at[way, step], (to_zp, to_zm)[way])
 
-    def ring_send(step):
-        for way in (0, 1):
+    def ring_send(step, ways=(0, 1)):
+        for way in ways:
             ring(step, way).start()
 
     def ring_wait(step):
@@ -157,6 +163,8 @@
     ring_send(0)
 
     load_stream.wait()
+    for copy in load_gains:
+        copy.wait()
     rows = FRAMES * BLOCK
     wide = own_stream[...].reshape(rows, D).astype(F32)
     mean_square = jnp.mean(wide * wide, axis=-1, keepdims=True)
@@ -171,6 +179,11 @@
     for m in range(2):
         other_part(m).start()
     ring_send(1)
+
+    for j in range(N_ROW):
+        gain_col[j] = jnp.broadcast_to(mlp_gain[:, j * LANES : (j + 1) * LANES], (LANES, LANES)).T
+    ring_wait(0)
+    ring_send(2)
 
     wait_slabs(0)
     wait_slabs(2)
@@ -251,6 +264,15 @@
         for m in ms:
             gather(f, m, True).wait_recv()
 
+    def fold(slot, *kinds):
+        zz = (z + slot + N_Z - OWN) % N_Z
+        for n in kinds:
+            for m in range(2):
+                gain = gain_col[2 * zz + m]
+                for c in range(0, HID, LANES):
+                    at = (n, slot, slice(m * LANES, (m + 1) * LANES), slice(c, c + LANES))
+                    folded[at] = (wgu[at].astype(F32) * gain).astype(BF16)
+
     most = (N_Z - 1) * WROWS
 
     def mlp_most(f, t):
@@ -260,25 +282,20 @@
             v = full[j, f, span, :].astype(F32)
             total = total + v * v
         scale = lax.rsqrt(jnp.sum(total, axis=-1, keepdims=True) * (1.0 / D) + 1e-05)
-        for slot in range(N_Z):
-            zz = (z + slot + N_Z - OWN) % N_Z
-            for n in range(2):
-                v = full[2 * zz + n, f, span, :].astype(F32)
-                gain = mlp_gain[:, pl.ds(pl.multiple_of((2 * zz + n) * LANES, LANES), LANES)]
-                v = (v * scale * gain).astype(BF16)
-                if slot < N_Z - 1:
-                    tok[:, slot * 256 + n * LANES : slot * 256 + (n + 1) * LANES] = v
-                else:
-                    tok_last[f, span, n * LANES : (n + 1) * LANES] = v
+        scales[f, span, :] = jnp.broadcast_to(scale, (256, LANES))
+        zs_of = [(z + slot + N_Z - OWN) % N_Z for slot in range(N_Z - 1)]
+        values = jnp.concatenate([full[2 * zz + n, f, span, :] for zz in zs_of for n in range(2)], axis=1)
         for n in range(2):
-            weight = wgu[n, : N_Z - 1].reshape(most, HID)
-            acc[n, f, span, :] = jnp.dot(tok[...], weight, preferred_element_type=F32)
+            weight = folded[n, : N_Z - 1].reshape(most, HID)
+            acc[n, f, span, :] = jnp.dot(values, weight, preferred_element_type=F32)
 
     def mlp_rest(f, t):
         span = pl.ds(pl.multiple_of(t * 256, 256), 256)
-        last = tok_last[f, span, :]
-        gate = acc[0, f, span, :] + jnp.dot(last, wgu[0, N_Z - 1], preferred_element_type=F32)
-        up = acc[1, f, span, :] + jnp.dot(last, wgu[1, N_Z - 1], preferred_element_type=F32)
+        zz = (z + N_Z - 1 - OWN) % N_Z
+        last = jnp.concatenate([full[2 * zz, f, span, :], full[2 * zz + 1, f, span, :]], axis=1)
+        scale = scales[f, span, 0:1]
+        gate = (acc[0, f, span, :] + jnp.dot(last, folded[0, N_Z - 1], preferred_element_type=F32)) * scale
+        up = (acc[1, f, span, :] + jnp.dot(last, folded[1, N_Z - 1], preferred_element_type=F32)) * scale
         hid[f, span, :] = (gate / (1.0 + jnp.exp(-gate)) * up).astype(BF16)
 
     load_table.wait()
@@ -290,39 +307,45 @@
         copy.wait()
     mixer_filter(0)
     g_send(0, 0, 1, 2, 9)
-    ring_wait(0)
-    ring_send(2)
+    ring_wait(1)
+    ring_send(3)
     wait_slabs(1)
     mixer_columns(1)
     mixer_rows(1)
     mixer_filter(1)
     g_send(1, 0, 1, 2, 9)
-    ring_wait(1)
-    ring_send(3)
+    fold(OWN, 0, 1)
+    fold(OWN - 1, 0, 1)
+    fold(OWN + 1, 0, 1)
+    ring_wait(2)
+    ring_send(4)
     g_wait(0, 0, 1)
     g_send(0, 3, 4, 10, 11)
+    g_wait(1, 0, 1)
+    g_send(1, 3, 4, 10, 11)
     g_wait(0, 2)
     g_send(0, 5, 6, 12)
-    ring_wait(2)
-    ring_send(4)
-    g_wait(1, 0, 1)
-    g_send(1, 3, 4, 10, 11)
     g_wait(1, 2)
     g_send(1, 5, 6, 12)
     ring_wait(3)
     ring_send(5)
     g_wait(0, 3, 4)
     g_send(0, 7, 8, 13, 14)
+    fold(OWN - 2, 0, 1)
+    fold(OWN + 2, 0, 1)
+    g_wait(1, 3, 4)
+    g_send(1, 7, 8, 13, 14)
+    ring_wait(4)
+    ring_send(6, (0,))
     g_wait(0, 5, 6)
     g_send(0, 15, 16)
-    ring_wait(4)
     ring_wait(5)
-    ring_send(6)
+    ring_send(6, (1,))
     ring_send(7)
-    g_wait(1, 3, 4)
-    g_send(1, 7, 8, 13, 14)
     g_wait(0, 7, 8)
     g_send(0, 17, 18)
+    fold(OWN - 3, 0, 1)
+    fold(OWN + 3, 0, 1)
     g_wait(0, *range(9, 19))
 
     def tiles(part_of, f, lo, hi):
@@ -338,10 +361,13 @@
     tiles(mlp_most, 0, 2, 4)
     g_wait(1, 7, 8)
     g_send(1, 17, 18)
+    g_wait(1, *range(9, 19))
+    tiles(mlp_most, 1, 0, 4)
     ring_wait(6)
-    tiles(mlp_rest, 0, 0, 4)
     ring_wait(7)
     ring_send(8)
+    fold(N_Z - 1, 0, 1)
+    tiles(mlp_rest, 0, 0, 4)
 
     q_same = lambda dy: ((y + dy + 4) % 4) * 2 + xh
     q_diff = lambda dy: ((y + dy + 4) % 4) * 2 + xo
@@ -416,6 +442,11 @@
         y5_tx[g, 1] = jnp.concatenate([total[: BLOCK // 2], second], axis=0).astype(BF16)
         reduce_copy(g, 8).start()
 
+    def out_copy(g):
+        f, off = place(g)
+        cols = pl.ds(pl.multiple_of((z + off + N_Z) % N_Z * WROWS, WROWS), WROWS)
+        return pltpu.make_async_copy(out.at[f, :, cols], out_ref.at[f, :, cols], outs.at[g])
+
     def stage4(g):
         f, off = place(g)
         zz = (z + off + N_Z) % N_Z
@@ -427,6 +458,7 @@
         got = jnp.concatenate([full[2 * zz, f, mine, :], full[2 * zz + 1, f, mine, :]], axis=1)
         cols = pl.ds(pl.multiple_of(zz * 256, 256), 256)
         out[f, :, cols] = (got.astype(F32) + total).astype(BF16)
+        out_copy(g).start()
 
     def step(g, _):
         for n, when in enumerate((4, 9)):
@@ -452,16 +484,6 @@
 
         @pl.when(g == 0)
         def _():
-            g_wait(1, *range(9, 19))
-            tiles(mlp_most, 1, 0, 2)
-
-        @pl.when(g == 1)
-        def _():
-            tiles(mlp_most, 1, 2, 3)
-
-        @pl.when(g == 2)
-        def _():
-            tiles(mlp_most, 1, 3, 4)
             tiles(mlp_rest, 1, 0, 4)
 
         return 0
@@ -486,6 +508,7 @@
     def drain_reduce(g, _):
         for m in range(9):
             reduce_copy(g, m).wait_send()
+        out_copy(g).wait()
         return 0
 
     lax.fori_loop(0, STEPS, drain_reduce, 0)
@@ -493,10 +516,12 @@
 
 def body(stream, mixer_gain, spectrum, mlp_gain, gate_weight, up_weight, down_weight):
     any_spec = pl.BlockSpec(memory_space=pl.ANY)
-    vmem_spec = pl.BlockSpec(memory_space=pltpu.VMEM)
     dma = pltpu.SemaphoreType.DMA
     scratch = [
+        pltpu.VMEM((FRAMES, BLOCK, D), BF16),
         pltpu.VMEM((1152, 256), BF16),
+        pltpu.VMEM((1, D), F32),
+        pltpu.VMEM((1, D), F32),
         pltpu.VMEM((FRAMES, BLOCK, D), BF16),
         pltpu.VMEM((N_ROW, FRAMES, BLOCK, LANES), BF16),
         pltpu.VMEM((N_ROW, 2, BLOCK, LANES), BF16),
@@ -510,8 +535,9 @@
         pltpu.VMEM((N_ROW, FRAMES, TOKENS, LANES), BF16),
         pltpu.VMEM((2, N_Z, WROWS, HID), BF16),
         pltpu.VMEM((N_Z, WROWS, HID), BF16),
-        pltpu.VMEM((256, D - WROWS), BF16),
-        pltpu.VMEM((FRAMES, TOKENS, WROWS), BF16),
+        pltpu.VMEM((N_ROW, LANES, LANES), F32),
+        pltpu.VMEM((2, N_Z, WROWS, HID), BF16),
+        pltpu.VMEM((FRAMES, TOKENS, LANES), F32),
         pltpu.VMEM((2, FRAMES, TOKENS, HID), F32),
         pltpu.VMEM((FRAMES, TOKENS, HID), BF16),
         pltpu.VMEM((LIVE, 512, CCOLS), F32),
@@ -527,7 +553,8 @@
         pltpu.VMEM((STEPS, BLOCK, CCOLS), BF16),
         pltpu.VMEM((STEPS, 2, BLOCK, CCOLS), BF16),
         pltpu.VMEM((STEPS, 2, BLOCK, CCOLS), BF16),
-        dma((5,)),
+        dma((7,)),
+        dma((STEPS,)),
         dma((4, N_ROW)),
         dma((4, N_ROW)),
         dma((2,)),
@@ -542,8 +569,8 @@
     result = pl.pallas_call(
         kernel,
         out_shape=jax.ShapeDtypeStruct((FRAMES, BLOCK, D), BF16),
-        in_specs=[any_spec, vmem_spec, any_spec, vmem_spec] + [any_spec] * 4,
-        out_specs=vmem_spec,
+        in_specs=[any_spec] * 8,
+        out_specs=any_spec,
         scratch_shapes=scratch,
         compiler_params=pltpu.CompilerParams(
             collective_id=0, has_side_effects=True, vmem_limit_bytes=62 * 2**20

time: 113 us -> 109 us (0.965)
  Pallas kernels: 110 us -> 106 us
    pallas_call x1, Pallas kernels: 110 us -> 106 us  [body(): pl.pallas_call(kernel, out_shape=jax.ShapeDtypeStruct((FRAMES, BLOCK, D),...]
where the time goes in v3:
time: 109 us; the launch traced here: 108 us
  Pallas kernels  106 us (97%)
  local copies, waits for them, and re-layouts  1.88 us (2%)
    pallas_call x1, Pallas kernels, body(): pl.pallas_call(kernel, out_shape=jax.ShapeDtypeStruct((FRAMES, BLOCK, D),...  106 us

profile of v3, /device:TPU:1, one launch (start us, length us, event | category | flops | bytes accessed | tf_op | source)
XLA Modules:
  0.0 108.0 jit_solution(11521772812947855453)
XLA Ops:
  0.0 106.2 %shard_map.82 = bf16[2,64,2048]{2,1,0:T(8,128)(2,1)} custom-call(bf16[2,64,2048]{2,1,0:T(8,128)(2,1)} %bitcast.7, f32[1,2048]{1,0:T(1,128)} %mixer_gain_ref.1, bf16[2,64,2048]{2,1,0:T(8,128)(2,1)} %bitcast.8, f32[1,2048]{1,0:T(1,128)} %mlp_gain_ref.1, bf16[256,512]{1,0:T(8,128)(2,1)} %bitcast.9, bf16[256,512]{1,0:T(8,128)(2,1)} %bitcast.10, ...), custom_call_target="tpu_custom_call" | custom-call | flops 14000000000 | bytes 6291456 | tf_op jit(solution)/shard_map/pallas_call | solution.py:569
  106.2 1.9 %copy.10 = bf16[1,2,2,32,2048]{4,3,2,1,0:T(8,128)(2,1)} copy(bf16[1,2,2,32,2048]{4,3,2,1,0:T(8,128)(2,1)} %bitcast.6) | data formatting | bytes 1048576

commit v4 on v3

--- a/solution.py
+++ b/solution.py
@@ -95,7 +95,7 @@
         pl.semaphore_signal(barrier, inc=1, device_id=(1 - seg, z, j), device_id_type=MESH)
         return 0
 
-    lax.fori_loop(0, N_ROW, greet, 0)
+    lax.fori_loop(0, N_ROW, greet, 0, unroll=True)
     for to in (to_yp, to_ym, to_x, to_sib, to_zp, to_zm):
         pl.semaphore_signal(barrier, inc=1, device_id=to, device_id_type=MESH)
     pl.semaphore_wait(barrier, N_ROW + 6)
@@ -118,7 +118,7 @@
             slab(kind, (me + j) % N_ROW).start()
             return 0
 
-        lax.fori_loop(0, N_ROW, step, 0)
+        lax.fori_loop(0, N_ROW, step, 0, unroll=True)
 
     def wait_slabs(kind):
         def step(j, _):
@@ -126,7 +126,7 @@
             remote(ref, ref, a2a_s.at[kind, j], a2a_r.at[kind, j], (1 - seg, z, j)).wait_recv()
             return 0
 
-        lax.fori_loop(0, N_ROW, step, 0)
+        lax.fori_loop(0, N_ROW, step, 0, unroll=True)
 
     def other_part(m, recv=False):
         to, slots = ((to_zp, pl.ds(0, N_ROW // 2)), (to_zm, pl.ds(N_ROW // 2, N_ROW // 2)))[m]
@@ -461,7 +461,7 @@
         out_copy(g).start()
 
     def step(g, _):
-        for n, when in enumerate((4, 9)):
+        for n, when in enumerate((5, 10)):
 
             @pl.when(g == when)
             def _(n=n):

time: 109 us -> 108 us (level)
  no operation moved by 1% of the time
where the time goes in v4:
time: 108 us; the launch traced here: 107 us
  Pallas kernels  105 us (97%)
  local copies, waits for them, and re-layouts  1.88 us (2%)
    pallas_call x1, Pallas kernels, body(): pl.pallas_call(kernel, out_shape=jax.ShapeDtypeStruct((FRAMES, BLOCK, D),...  105 us

profile of v4, /device:TPU:1, one launch (start us, length us, event | category | flops | bytes accessed | tf_op | source)
XLA Modules:
  0.0 107.3 jit_solution(11090696811430884096)
XLA Ops:
  0.0 105.4 %shard_map.82 = bf16[2,64,2048]{2,1,0:T(8,128)(2,1)} custom-call(bf16[2,64,2048]{2,1,0:T(8,128)(2,1)} %bitcast.7, f32[1,2048]{1,0:T(1,128)} %mixer_gain_ref.1, bf16[2,64,2048]{2,1,0:T(8,128)(2,1)} %bitcast.8, f32[1,2048]{1,0:T(1,128)} %mlp_gain_ref.1, bf16[256,512]{1,0:T(8,128)(2,1)} %bitcast.9, bf16[256,512]{1,0:T(8,128)(2,1)} %bitcast.10, ...), custom_call_target="tpu_custom_call" | custom-call | flops 14000000000 | bytes 6291456 | tf_op jit(solution)/shard_map/pallas_call | solution.py:569
  105.4 1.9 %copy.10 = bf16[1,2,2,32,2048]{4,3,2,1,0:T(8,128)(2,1)} copy(bf16[1,2,2,32,2048]{4,3,2,1,0:T(8,128)(2,1)} %bitcast.6) | data formatting | bytes 1048576
